TPU v7x, 512 devices: a whole 4x8x8 slice. The times are simulated.
512 devices in a mesh: mem: 8 (over x, core), col: 64 (over z, y).
Axes of the slice: x: 4, y: 8, z: 8, core: 2. Of those that a mesh axis runs over, the one named last changes fastest.
Arguments:
- controls: bfloat16 [8, 127, 98304], P('mem', None, 'col'), may hold values from -6 to 6
- perturbations: bfloat16 [8, 127, 98304], P('mem', None, 'col'), may hold values from -6 to 6
- vertical_filter: bfloat16 [127, 127], replicated, may hold values from -4 to 4
- scales: float32 [127], replicated, may hold values from 16 to 48
- level_counts: int32 [64], replicated, may hold values from 1 to 4, 127 in all
- weight_index: int32 [8], P('mem'), may hold values from 0 to 9
- member_weights: float32 [10], replicated, may hold values from 0.1 to 0.6
Outputs:
- increment: float32 [127, 98304], P(None, 'col')
- slab_increment: float32 [256, 64, 1536], P('col', None, 'mem')
Inputs may be any that keep to these rules, and one draw needn't show every extreme that they name: `level_counts`: the counts sum to 127; some tile owns exactly 4 levels.
All inputs are finite; a program needn't handle non-finite values.
Results may differ from a plain program's by a relative error of at most 0.0062.
Values may be sent and summed in bfloat16 or wider, within the bound.
A program may use at most 64 MiB of HBM per device.

v0:
```python
import jax
import jax.numpy as jnp
from jax import lax
from jax.sharding import PartitionSpec as P

NLON = 1536
HALF = 24
NW = 10


def on_device(
    controls, perturbations, vertical_filter, scales, level_counts, weight_index, member_weights
):
    tiles = lax.axis_size("col")
    levels = vertical_filter.shape[0]
    slot_count = 2 * ((levels + tiles - 1) // tiles)
    row_count = tiles * slot_count
    band = controls.shape[2] // NLON
    latitude = band * tiles
    blocks = NLON // 128
    tile_ids = jnp.arange(tiles)
    earlier = (tile_ids[None, :] < tile_ids[:, None]).astype(jnp.int32)
    starts = jnp.sum(earlier * level_counts[None, :], axis=1)
    row_ids = jnp.arange(row_count)
    position = row_ids % slot_count
    target = jnp.repeat(starts, slot_count) + position
    filled = position < jnp.repeat(level_counts, slot_count)
    level_ids = jnp.arange(levels)
    placing = (filled[:, None] & (level_ids[None, :] == target[:, None])).astype(jnp.float32)
    placing_narrow = placing.astype(jnp.bfloat16)
    permuted = jnp.dot(placing_narrow, vertical_filter, preferred_element_type=jnp.float32).astype(
        jnp.bfloat16
    )
    lifted = jnp.einsum(
        "rl,mlc->mrc", permuted, controls, preferred_element_type=jnp.float32
    ).astype(jnp.bfloat16)
    placed_perturb = jnp.einsum(
        "rl,mlc->mrc", placing_narrow, perturbations, preferred_element_type=jnp.float32
    ).astype(jnp.bfloat16)
    owned = lax.dynamic_slice_in_dim(placing, lax.axis_index("col") * slot_count, slot_count, 0)
    occupied = jnp.sum(owned, axis=1)
    slot_scale = jnp.dot(owned, scales, precision=lax.Precision.HIGHEST) + (1.0 - occupied)
    width = slot_scale[:, None]
    offsets = jnp.arange(-HALF, HALF + 1).astype(jnp.float32)
    normal = jnp.sqrt(jnp.sum(jnp.exp(-(offsets * offsets) / (width * width)), axis=1))
    width3 = slot_scale[:, None, None]
    normal3 = normal[:, None, None]

    def kernel(distance):
        raw = jnp.exp(-(distance * distance) / (2.0 * width3 * width3)) / normal3
        return jnp.where(jnp.abs(distance) <= HALF, raw, jnp.float32(0.0)).astype(jnp.bfloat16)

    source = jnp.arange(128)[:, None]
    dest = jnp.arange(128)[None, :]
    lon_before = kernel((dest - source + 128).astype(jnp.float32)[None])
    lon_same = kernel((dest - source).astype(jnp.float32)[None])
    lon_after = kernel((dest - source - 128).astype(jnp.float32)[None])
    lat_rows = jnp.arange(latitude)
    lat_matrix = kernel((lat_rows[:, None] - lat_rows[None, :]).astype(jnp.float32)[None])
    selector = (weight_index[:, None] == jnp.arange(NW)[None, :]).astype(jnp.float32)
    betas = jnp.dot(selector, member_weights, precision=lax.Precision.HIGHEST)
    arrived = lax.all_to_all(lifted[0], "col", split_axis=0, concat_axis=1, tiled=True)
    arrived_perturb = lax.all_to_all(
        placed_perturb[0], "col", split_axis=0, concat_axis=1, tiled=True
    )
    field = arrived[None]
    perturb = arrived_perturb[None]
    items = field.shape[0]
    horizontal_items = field.shape[0]
    grid = field.reshape(horizontal_items, slot_count, latitude, blocks, 128)
    before = jnp.roll(grid, 1, axis=3)
    after = jnp.roll(grid, -1, axis=3)
    along = jnp.einsum("qsiba,sac->qsibc", before, lon_before, preferred_element_type=jnp.float32)
    along = along + jnp.einsum(
        "qsiba,sac->qsibc", grid, lon_same, preferred_element_type=jnp.float32
    )
    along = along + jnp.einsum(
        "qsiba,sac->qsibc", after, lon_after, preferred_element_type=jnp.float32
    )
    along = along.astype(jnp.bfloat16)
    smooth = jnp.einsum("sij,qsjbc->qsibc", lat_matrix, along, preferred_element_type=jnp.float32)
    smooth = smooth.reshape(horizontal_items, slot_count, latitude, NLON)
    product = (perturb.astype(jnp.float32).reshape(items, slot_count, latitude, NLON) * smooth)[0]
    slab_local = betas[0] * product
    slab_increment = lax.psum_scatter(slab_local, "mem", scatter_dimension=2, tiled=True)
    selecting = placing.T
    returned = lax.all_to_all(slab_local, "col", split_axis=1, concat_axis=0, tiled=True)
    columns = jnp.dot(
        selecting, returned.reshape(row_count, band * NLON), precision=lax.Precision.HIGHEST
    )
    increment = lax.psum(columns, "mem")
    return (increment, slab_increment)


def solution(mesh):
    return jax.shard_map(
        on_device,
        mesh=mesh,
        in_specs=(P("mem", None, "col"), P("mem", None, "col"), P(), P(), P(), P("mem"), P()),
        out_specs=(P(None, "col"), P("col", None, "mem")),
        check_vma=False,
    )
```

profile of v0, /device:TPU:1, one launch (start us, length us, event | category | flops | bytes accessed | tf_op | source)
XLA Modules:
  0.0 221.6 jit_solution(15295517255990789751)
XLA Ops:
  7.2 0.8 select_reduce_fusion
  8.2 0.7 broadcast_in_dim.63
  9.1 1.3 fusion.1
  10.4 1.1 all_to_all.35
  11.4 17.1 %all-to-all-start.1 = ((bf16[64,4,1536]{2,1,0:T(4,128)(2,1)}), bf16[64,4,1536]{2,1,0:T(4,128)(2,1)S(1)}, u32[]{:S(2)}, u32[]{:S(2)}) async-start(bf16[64,4,1536]{2,1,0:T(4,128)(2,1)} %all_to_all.35), calls=%async_computation.1 | async-start | bytes 1572864 | tf_op jit(solution)/shard_map/all_to_all | solution.py:62
  29.1 1.1 all_to_all.33
  31.6 18.9 %all-to-all-done.1 = bf16[64,4,1536]{2,1,0:T(4,128)(2,1)S(1)} async-done(((bf16[64,4,1536]{2,1,0:T(4,128)(2,1)}), bf16[64,4,1536]{2,1,0:T(4,128)(2,1)S(1)}, u32[]{:S(2)}, u32[]{:S(2)}) %all-to-all-start.1) | async-done | bytes 786464 | tf_op jit(solution)/shard_map/all_to_all | solution.py:62
  50.4 7.9 %all-to-all-start = ((bf16[64,4,1536]{2,1,0:T(4,128)(2,1)}), bf16[64,4,1536]{2,1,0:T(4,128)(2,1)}, u32[]{:S(2)}, u32[]{:S(2)}) async-start(bf16[64,4,1536]{2,1,0:T(4,128)(2,1)} %all_to_all.33), calls=%async_computation | async-start | bytes 1572864 | tf_op jit(solution)/shard_map/all_to_all | solution.py:63
  58.3 0.6 fusion.67
  59.0 0.5 reshape.249
  59.5 1.5 reshape.246
  61.5 0.5 copy.52
  62.3 0.5 copy.53
  63.2 0.8 copy-done.1
  64.0 1.9 fusion.12
  65.8 3.2 %convolution_bitcast_fusion = f32[1,4,64,12,128]{4,2,3,1,0:T(8,128)} fusion(f32[4,128,64,12]{1,2,3,0:T(8,128)S(1)} %fusion.5, f32[4,128,64,12]{1,2,3,0:T(8,128)} %fusion.12, bf16[1,4,64,1,128]{4,2,3,1,0:T(8,128)(2,1)S(1)} %copy.54, bf16[1,4,64,11,128]{4,2,3,1,0:T(8,128)(2,1)S(1)} %copy.53, f32[128,128]{1,0:T(8,128)S(1)} %multiply_negate_fusion, ...), kind=kOutput, calls=%fused_computation.7 | convolution fusion | flops 154075136 | bytes 5607456 | tf_op jit(solution)/shard_map/sij,qsjbc->qsibc/dot_general | solution.py:81
  69.1 2.3 %copy.37 = f32[1,4,64,12,128]{4,3,2,1,0:T(8,128)S(1)} copy(f32[1,4,64,12,128]{4,2,3,1,0:T(8,128)} %convolution_bitcast_fusion) | data formatting | bytes 3145728 | tf_op jit(solution)/shard_map/sij,qsjbc->qsibc/transpose | solution.py:81
  71.4 1.4 reshape.235
  72.8 6.2 %all-to-all-done = bf16[64,4,1536]{2,1,0:T(4,128)(2,1)} async-done(((bf16[64,4,1536]{2,1,0:T(4,128)(2,1)}), bf16[64,4,1536]{2,1,0:T(4,128)(2,1)}, u32[]{:S(2)}, u32[]{:S(2)}) %all-to-all-start) | async-done | bytes 786464 | tf_op jit(solution)/shard_map/all_to_all | solution.py:63
  79.0 2.5 %fusion.2 = f32[4,64,1536]{2,1,0:T(8,128)S(1)} fusion(f32[4,64,1536]{2,1,0:T(8,128)} %reshape.235, bf16[64,4,1536]{2,1,0:T(4,128)(2,1)} %all-to-all-done, f32[]{:T(128)} %fusion.67), kind=kLoop, calls=%fused_computation.5 | loop fusion | flops 1179648 | bytes 3932164 | tf_op jit(solution)/shard_map/mul | solution.py:84
  81.5 2.2 copy.38
  83.7 8.0 %all-to-all-start.2 = ((f32[4,64,1536]{2,0,1:T(4,128)}), f32[4,64,1536]{2,0,1:T(4,128)S(1)}, u32[]{:S(2)}, u32[]{:S(2)}) async-start(f32[4,64,1536]{2,0,1:T(4,128)} %copy.38), calls=%async_computation.2 | async-start | bytes 3145728 | tf_op jit(solution)/shard_map/all_to_all | solution.py:87
  91.9 2.7 %copy.47 = f32[4,64,1536]{1,0,2:T(4,128)} copy(f32[4,64,1536]{2,1,0:T(8,128)S(1)} %fusion.2) | data formatting | bytes 3145728
  94.6 4.2 %reshape.247 = f32[1536,256]{1,0:T(8,128)} reshape(f32[1536,4,64]{2,1,0:T(4,128)} %bitcast.87) | data formatting | bytes 3145728
  98.8 28.9 %all-to-all-done.2 = f32[4,64,1536]{2,0,1:T(4,128)S(1)} async-done(((f32[4,64,1536]{2,0,1:T(4,128)}), f32[4,64,1536]{2,0,1:T(4,128)S(1)}, u32[]{:S(2)}, u32[]{:S(2)}) %all-to-all-start.2) | async-done | bytes 1572896 | tf_op jit(solution)/shard_map/all_to_all | solution.py:87
  127.8 0.5 reshape.236
  128.3 1.7 fusion.82
  130.0 8.6 %reduce-scatter.4.cloned.1.call-done = f32[192,256]{1,0:T(8,128)} async-done(((f32[1536,256]{1,0:T(8,128)}), f32[192,256]{1,0:T(8,128)}) %reduce-scatter.4.cloned.1.call-update) | async-done | bytes 196624
  138.6 1.1 reshape.248
  139.7 0.9 copy.48
  140.6 72.1 %all-reduce.2.cloned.1.call-done = f32[127,1536]{1,0:T(8,128)} async-done(((f32[127,1536]{1,0:T(8,128)}), f32[127,1536]{1,0:T(8,128)}) %all-reduce.2.cloned.1.call-update) | async-done | bytes 780304 | tf_op jit(solution)/shard_map/psum | solution.py:91
  212.7 2.1 copy.60
  (38 shorter events, 3.0 us)
Async XLA Ops:
  7.2 1.9 copy-start
  10.4 18.2 %copy-start.2 = (bf16[1,127,1536]{2,1,0:T(8,128)(2,1)S(1)}, bf16[1,127,1536]{2,1,0:T(8,128)(2,1)}, u32[]{:S(2)}) copy-start(bf16[1,127,1536]{2,1,0:T(8,128)(2,1)} %param.8) | copy-start | bytes 1170436
  11.4 39.0 %all-to-all-start.1 = ((bf16[64,4,1536]{2,1,0:T(4,128)(2,1)}), bf16[64,4,1536]{2,1,0:T(4,128)(2,1)S(1)}, u32[]{:S(2)}, u32[]{:S(2)}) async-start(bf16[64,4,1536]{2,1,0:T(4,128)(2,1)} %all_to_all.35), calls=%async_computation.1 | async-start | bytes 1572864 | tf_op jit(solution)/shard_map/all_to_all | solution.py:62
  28.6 2.6 %copy-start.3 = (f32[127]{0:T(128)S(1)}, f32[127]{0:T(128)}, u32[]{:S(2)}) copy-start(f32[127]{0:T(128)} %param.10) | copy-start | bytes 1528
  29.0 29.3 %copy-start.4 = (f32[10]{0:T(128)S(1)}, f32[10]{0:T(128)}, u32[]{:S(2)}) copy-start(f32[10]{0:T(128)} %param.13) | copy-start | bytes 124
  50.4 28.5 %all-to-all-start = ((bf16[64,4,1536]{2,1,0:T(4,128)(2,1)}), bf16[64,4,1536]{2,1,0:T(4,128)(2,1)}, u32[]{:S(2)}, u32[]{:S(2)}) async-start(bf16[64,4,1536]{2,1,0:T(4,128)(2,1)} %all_to_all.33), calls=%async_computation | async-start | bytes 1572864 | tf_op jit(solution)/shard_map/all_to_all | solution.py:63
  62.8 1.2 copy-start.1
  83.7 44.1 %all-to-all-start.2 = ((f32[4,64,1536]{2,0,1:T(4,128)}), f32[4,64,1536]{2,0,1:T(4,128)S(1)}, u32[]{:S(2)}, u32[]{:S(2)}) async-start(f32[4,64,1536]{2,0,1:T(4,128)} %copy.38), calls=%async_computation.2 | async-start | bytes 3145728 | tf_op jit(solution)/shard_map/all_to_all | solution.py:87
  91.7 47.0 %reduce-scatter.4.cloned.1.call-start = ((), (), s32[]{:S(2)}) async-start(), calls=%async_computation.5 | async-start | bytes 1769472
  98.8 113.9 %all-reduce.2.cloned.1.call-start = ((), (), s32[]{:S(2)}) async-start(), calls=%async_computation.4 | async-start | bytes 1572864 | tf_op jit(solution)/shard_map/psum | solution.py:91
Sparse Core Ops, SparseCore 0:
  98.9 39.6 reduce-scatter.3
  141.5 71.1 all-reduce.1
where the time goes:
time: 223 us; the launch traced here: 222 us
  waiting for transfers between devices  135 us (61%)
  starting transfers between devices  33.2 us (15%)
  local copies, waits for them, and re-layouts  25.1 us (11%)
  between operations  15 us (7%)
  matrix products  9.02 us (4%)
  other arithmetic  4.58 us (2%)
    psum x1, waiting for transfers between devices, on_device(): increment = lax.psum(columns, 'mem')  72.1 us
    all_to_all x1, waiting for transfers between devices, on_device(): lax.all_to_all(slab_local, 'col', split_axis=1, concat_axis=0, tiled=True)  28.9 us
    all_to_all x1, waiting for transfers between devices, on_device(): lax.all_to_all(lifted[0], 'col', split_axis=0, concat_axis=1, tiled=True)  18.9 us
    all_to_all x1, starting transfers between devices, on_device(): lax.all_to_all(lifted[0], 'col', split_axis=0, concat_axis=1, tiled=True)  17.1 us
    unnamed x19, local copies, waits for them, and re-layouts  12.8 us
    unnamed x3, waiting for transfers between devices  8.66 us
    all_to_all x1, starting transfers between devices, on_device(): lax.all_to_all(slab_local, 'col', split_axis=1, concat_axis=0, tiled=True)  7.97 us
    all_to_all x1, starting transfers between devices, on_device(): lax.all_to_all(placed_perturb[0], 'col', split_axis=0, concat_axis=1, til...  7.88 us
  transfers between devices with their start and end apart: 5, of which 5 were waited for; matrix products, arithmetic and copies ran while one was open for 12% of the time, Pallas kernels for 0%

commit v1 on v0

v1 whole, which is shorter than its diff:
```python
import jax
import jax.numpy as jnp
from jax import lax
from jax.experimental import pallas as pl
from jax.experimental.pallas import tpu as pltpu
from jax.sharding import PartitionSpec as P

LEV = 127
NLON = 1536
HALF = 24
MEM = 8
COL = 64
SIDE = 8
PARTS = 3
PAD = 32
MESH = pl.DeviceIdType.MESH
F32 = jnp.float32
BF16 = jnp.bfloat16


def taps_rows(width):
    rows = lax.broadcasted_iota(jnp.int32, (PAD, 128), 0).astype(F32)
    raw = jnp.exp(-(rows * rows) / (2.0 * width * width))
    squares = jnp.where(rows <= HALF, jnp.exp(-(rows * rows) / (width * width)), 0.0)
    normal = jnp.sqrt(2.0 * jnp.sum(squares, axis=0, keepdims=True) - 1.0)
    return (raw / normal).astype(BF16).astype(F32)


def placing_matrix(counts):
    row = lax.broadcasted_iota(jnp.int32, (COL * 8, 1), 0)
    tile, slot, half = row // 8, lax.rem(row, 4), lax.rem(row // 4, 2)
    lane = lax.broadcasted_iota(jnp.int32, (COL * 8, COL), 1)
    start = jnp.sum(jnp.where(lane < tile, counts, 0.0), axis=1, keepdims=True)
    count = jnp.sum(jnp.where(lane == tile, counts, 0.0), axis=1, keepdims=True)
    slot_f = slot.astype(F32)
    target = jnp.where(slot_f < count, start + slot_f + 128.0 * half.astype(F32), -1.0)
    wide = lax.broadcasted_iota(jnp.int32, (COL * 8, 256), 1).astype(F32)
    return jnp.where(wide == target, 1.0, 0.0).astype(BF16)


def exchange_kernel(
    controls, perturb, vertical, scales, counts, index, weights,
    gathered_out, slab_out,
    lifted, width_row, taps, along, arrived, padded, smooth, back, scaled,
    terms, sums, total, gathered, pair, placing, slab_send, slab_recv,
    send_sems, recv_sems,
):
    m = lax.axis_index("mem")
    c = lax.axis_index("col")
    z, y = c // SIDE, lax.rem(c, SIDE)

    barrier = pltpu.get_barrier_semaphore()

    def greet(k, carry):
        pl.semaphore_signal(
            barrier, inc=1, device_id=(m, lax.rem(c + k, COL)), device_id_type=MESH
        )
        return carry

    lax.fori_loop(1, COL, greet, 0)
    for k in range(1, MEM):
        pl.semaphore_signal(barrier, inc=1, device_id=(lax.rem(m + k, MEM), c), device_id_type=MESH)

    width_row[...] = jnp.full((1, 128), 16.0, F32)
    width_row[:, :LEV] = scales[...]
    taps[...] = taps_rows(width_row[...])

    def lift(matrix, source, t):
        block = jnp.dot(
            matrix, source[0, :, pl.ds(pl.multiple_of(t * 128, 128), 128)],
            preferred_element_type=F32,
        )
        return block

    filter_rows = vertical[...]

    def lift_block(t, carry):
        block = lift(filter_rows, controls, t).astype(BF16).astype(F32)
        lifted[pl.ds(pl.multiple_of(PAD + t * 128, 32), 128), :] = block.T
        return carry

    lax.fori_loop(0, NLON // 128, lift_block, 0)
    lifted[pl.ds(0, PAD), :] = lifted[pl.ds(NLON, PAD), :]
    lifted[pl.ds(PAD + NLON, PAD), :] = lifted[pl.ds(PAD, PAD), :]
    padded[pl.ds(0, HALF)] = jnp.zeros((HALF, 8, 128), F32)
    padded[pl.ds(HALF + COL, HALF)] = jnp.zeros((HALF, 8, 128), F32)

    pl.semaphore_wait(barrier, COL - 1 + MEM - 1)

    def weight_rows():
        return [jnp.broadcast_to(taps[k : k + 1, :], (8, 128)) for k in range(HALF + 1)]

    def send_col(kind, s, src, dst, row):
        pltpu.make_async_remote_copy(
            src_ref=src, dst_ref=dst,
            send_sem=send_sems.at[kind, s], recv_sem=recv_sems.at[kind, s],
            device_id=(m, row), device_id_type=MESH,
        ).start()

    def send_group(kind, s, source, dest, group, other):
        for r in range(SIDE):
            row = group * SIDE + lax.rem(y + r, SIDE)
            if r == 0:
                @pl.when(other)
                def _():
                    send_col(kind, s, source.at[s, row], dest.at[s, c], row)
            else:
                send_col(kind, s, source.at[s, row], dest.at[s, c], row)

    def lon_step(it, carry):
        w = weight_rows()
        s, k = it // SIDE, lax.rem(it, SIDE)
        group = lax.rem(z + 4 + k, SIDE)
        base = PAD + group * 192 + s * 64
        for b in range(SIDE):
            at = pl.multiple_of(base + 8 * b, 8)
            acc = w[0] * lifted[pl.ds(at, 8), :]
            for tap in range(1, HALF + 1):
                acc = acc + w[tap] * (lifted[pl.ds(at - tap, 8), :] + lifted[pl.ds(at + tap, 8), :])
            along[s, group * SIDE + b] = acc.astype(BF16)
        send_group(0, s, along, arrived, group, k != 4)
        return carry

    lax.fori_loop(0, PARTS * SIDE, lon_step, 0)

    beta = weights[index[0]]
    identity = jnp.where(
        lax.broadcasted_iota(jnp.int32, (128, LEV), 0)
        == lax.broadcasted_iota(jnp.int32, (128, LEV), 1),
        1.0, 0.0,
    ).astype(BF16)

    def perturb_block(t, carry):
        block = lift(identity, perturb, t) * beta
        scaled[pl.ds(pl.multiple_of(t * 128, 128), 128), :] = block.T
        return carry

    lax.fori_loop(0, NLON // 128, perturb_block, 0)
    placing[...] = placing_matrix(counts[...])
    pair[pl.ds(64, 64), pl.ds(128, 128)] = jnp.zeros((64, 128), BF16)

    def wait_recv(kind, s, dest, count):
        ref = dest.at[s, pl.ds(0, count)]
        pltpu.make_async_remote_copy(
            src_ref=ref, dst_ref=ref,
            send_sem=send_sems.at[kind, s], recv_sem=recv_sems.at[kind, s],
            device_id=(m, c), device_id_type=MESH,
        ).wait_recv()

    def wait_send(kind, s, source, count):
        ref = source.at[s, pl.ds(0, count)]
        pltpu.make_async_remote_copy(
            src_ref=ref, dst_ref=ref,
            send_sem=send_sems.at[kind, s], recv_sem=recv_sems.at[kind, s],
            device_id=(m, c), device_id_type=MESH,
        ).wait_send()

    def lat_part(s, carry):
        wait_recv(0, s, arrived, COL - 1)
        arrived[s, c] = along[s, c]
        padded[pl.ds(HALF, COL)] = arrived[s].astype(F32)

        def lat_step(k, inner):
            w = weight_rows()
            group = lax.rem(z + 4 + k, SIDE)
            for r in range(SIDE):
                at = HALF + group * SIDE + r
                acc = w[0] * padded[at]
                for tap in range(1, HALF + 1):
                    acc = acc + w[tap] * (padded[at - tap] + padded[at + tap])
                smooth[s, group * SIDE + r] = acc.astype(BF16)
            send_group(1, s, smooth, back, group, k != 4)
            return inner

        lax.fori_loop(0, SIDE, lat_step, 0)
        return carry

    lax.fori_loop(0, PARTS, lat_part, 0)

    def product_part(s, carry):
        wait_recv(1, s, back, COL - 1)
        back[s, c] = smooth[s, c]

        def product_step(k, inner):
            j = lax.rem(m + 1 + k, MEM)
            field = back[s, pl.ds(j * SIDE, SIDE)].astype(F32).reshape(64, 128)
            rows = scaled[pl.ds(pl.multiple_of(j * 192 + s * 64, 64), 64), :]
            terms[s, j] = (field * rows).astype(BF16).reshape(8, 8, 128)

            @pl.when(k < MEM - 1)
            def _():
                pltpu.make_async_remote_copy(
                    src_ref=terms.at[s, j], dst_ref=sums.at[s, m],
                    send_sem=send_sems.at[2, s], recv_sem=recv_sems.at[2, s],
                    device_id=(j, c), device_id_type=MESH,
                ).start()

            return inner

        lax.fori_loop(0, MEM, product_step, 0)
        return carry

    def sum_part(s, carry):
        wait_recv(2, s, sums, MEM - 1)
        sums[s, m] = terms[s, m]
        acc = sums[s, 0].astype(F32)
        for k in range(1, MEM):
            acc = acc + sums[s, k].astype(F32)
        part = acc.astype(BF16)
        total[s] = part
        gathered[s, m] = part

        def spread(k, inner):
            pltpu.make_async_remote_copy(
                src_ref=total.at[s], dst_ref=gathered.at[s, m],
                send_sem=send_sems.at[3, s], recv_sem=recv_sems.at[3, s],
                device_id=(lax.rem(m + k, MEM), c), device_id_type=MESH,
            ).start()
            return inner

        lax.fori_loop(1, MEM, spread, 0)
        return carry

    def product_sum(s, carry):
        product_part(s, 0)

        @pl.when(s > 0)
        def _():
            sum_part(s - 1, 0)

        return carry

    lax.fori_loop(0, PARTS, product_sum, 0)
    sum_part(PARTS - 1, 0)

    pair[pl.ds(0, 64), pl.ds(0, 128)] = total[0].reshape(64, 128)
    pair[pl.ds(64, 64), pl.ds(0, 128)] = total[1].reshape(64, 128)
    pair[pl.ds(0, 64), pl.ds(128, 128)] = total[2].reshape(64, 128)
    slab_send[0] = (
        lax.dot_general(
            placing[...], pair[...], (((1,), (1,)), ((), ())), preferred_element_type=F32
        )
        .astype(BF16)
        .reshape(COL, 8, 128)
    )

    def slab_step(k, carry):
        group = lax.rem(z + 4 + k, SIDE)
        for r in range(SIDE):
            row = group * SIDE + lax.rem(y + r, SIDE)
            if r == 0:
                @pl.when(k != 4)
                def _():
                    send_col(4, 0, slab_send.at[0, row], slab_recv.at[0, c], row)
            else:
                send_col(4, 0, slab_send.at[0, row], slab_recv.at[0, c], row)
        return carry

    lax.fori_loop(0, SIDE, slab_step, 0)

    def finish(s, carry):
        wait_recv(3, s, gathered, MEM - 1)
        gathered_out[s] = gathered[s]
        wait_send(0, s, along, COL - 1)
        wait_send(1, s, smooth, COL - 1)
        wait_send(2, s, terms, MEM - 1)
        wait_send(3, s, terms, MEM - 1)
        return carry

    lax.fori_loop(0, PARTS, finish, 0)
    wait_recv(4, 0, slab_recv, COL - 1)
    slab_recv[0, c] = slab_send[0, c]
    slab_out[...] = slab_recv[0]
    wait_send(4, 0, slab_send, COL - 1)


def exchange(controls, perturb, vertical, scales, counts, index, weights):
    block = (8, 128)
    vmem = pl.BlockSpec(memory_space=pltpu.VMEM)
    smem = pl.BlockSpec(memory_space=pltpu.SMEM)
    return pl.pallas_call(
        exchange_kernel,
        out_shape=(
            jax.ShapeDtypeStruct((PARTS, MEM, 8) + block, BF16),
            jax.ShapeDtypeStruct((COL,) + block, BF16),
        ),
        in_specs=[vmem, vmem, vmem, vmem, vmem, smem, smem],
        out_specs=(vmem, vmem),
        scratch_shapes=[
            pltpu.VMEM((PAD + NLON + PAD, 128), F32),
            pltpu.VMEM((1, 128), F32),
            pltpu.VMEM((PAD, 128), F32),
            pltpu.VMEM((PARTS, COL) + block, BF16),
            pltpu.VMEM((PARTS, COL) + block, BF16),
            pltpu.VMEM((HALF + COL + HALF,) + block, F32),
            pltpu.VMEM((PARTS, COL) + block, BF16),
            pltpu.VMEM((PARTS, COL) + block, BF16),
            pltpu.VMEM((NLON, 128), F32),
            pltpu.VMEM((PARTS, MEM, 8) + block, BF16),
            pltpu.VMEM((PARTS, MEM, 8) + block, BF16),
            pltpu.VMEM((PARTS, 8) + block, BF16),
            pltpu.VMEM((PARTS, MEM, 8) + block, BF16),
            pltpu.VMEM((128, 256), BF16),
            pltpu.VMEM((COL * 8, 256), BF16),
            pltpu.VMEM((1, COL) + block, BF16),
            pltpu.VMEM((1, COL) + block, BF16),
            pltpu.SemaphoreType.DMA((5, PARTS)),
            pltpu.SemaphoreType.DMA((5, PARTS)),
        ],
        compiler_params=pltpu.CompilerParams(
            collective_id=0, has_side_effects=True, vmem_limit_bytes=40 * 1024 * 1024
        ),
        name="exchange",
    )(controls, perturb, vertical, scales, counts, index, weights)


def arrange_kernel(gathered, slab, increment, slab_increment, rows):
    for t in range(NLON // 128):
        halves = [gathered[u % 3, u // 3].astype(F32).reshape(64, 128) for u in (2 * t, 2 * t + 1)]
        block = jnp.concatenate(halves, axis=0).T
        increment[:, pl.ds(t * 128, 128)] = block[:LEV]
    rows[...] = slab[...].astype(F32).reshape(COL * 8, 128)
    for q in range(4):
        slab_increment[q, :, pl.ds(0, 128)] = rows[pl.ds(q, COL, stride=8), :]
        slab_increment[q, :, pl.ds(128, 64)] = rows[pl.ds(4 + q, COL, stride=8), :][:, :64]


def arrange(gathered, slab):
    vmem = pl.BlockSpec(memory_space=pltpu.VMEM)
    return pl.pallas_call(
        arrange_kernel,
        out_shape=(
            jax.ShapeDtypeStruct((LEV, NLON), F32),
            jax.ShapeDtypeStruct((4, COL, 192), F32),
        ),
        in_specs=[vmem, vmem],
        out_specs=(vmem, vmem),
        scratch_shapes=[pltpu.VMEM((COL * 8, 128), F32)],
        compiler_params=pltpu.CompilerParams(vmem_limit_bytes=16 * 1024 * 1024),
        name="arrange",
    )(gathered, slab)


def on_device(
    controls, perturbations, vertical_filter, scales, level_counts, weight_index, member_weights
):
    vertical = jnp.pad(vertical_filter, ((0, 1), (0, 0)))
    gathered, slab = exchange(
        controls, perturbations, vertical, scales[None, :],
        level_counts.astype(F32)[None, :], weight_index, member_weights,
    )
    return arrange(gathered, slab)


def solution(mesh):
    return jax.shard_map(
        on_device,
        mesh=mesh,
        in_specs=(P("mem", None, "col"), P("mem", None, "col"), P(), P(), P(), P("mem"), P()),
        out_specs=(P(None, "col"), P("col", None, "mem")),
        check_vma=False,
    )
```

time: 223 us -> 61.8 us (0.28)
  waiting for transfers between devices: 135 us -> 0 us
  Pallas kernels: 0 us -> 56.8 us
  starting transfers between devices: 33.2 us -> 0 us
  local copies, waits for them, and re-layouts: 25.1 us -> 3.44 us
  between operations: 15 us -> 1.32 us
  matrix products: 9.02 us -> 0 us
  other arithmetic: 4.58 us -> 0.01 us
    psum x1 -> x0, waiting for transfers between devices: 72.1 us -> none  [on_device(): increment = lax.psum(columns, 'mem')]
    pallas_call x0 -> x2, Pallas kernels: none -> 56.8 us  [the longest x1 55.7 us: exchange(): pl.pallas_call(exchange_kernel, out_shape=(jax.ShapeDtypeStruct((PARTS, M...]
    all_to_all x3 -> x0, waiting for transfers between devices: 54 us -> none  [the longest x1 28.9 us: on_device(): lax.all_to_all(slab_local, 'col', split_axis=1, concat_axis=0, tiled=True)]
    all_to_all x3 -> x0, starting transfers between devices: 33 us -> none  [the longest x1 17.1 us: on_device(): lax.all_to_all(lifted[0], 'col', split_axis=0, concat_axis=1, tiled=True)]
    unnamed x19 -> x10, local copies, waits for them, and re-layouts: 12.8 us -> 2.64 us
    dot_general x7 -> x0, matrix products: 9.02 us -> none  [the longest x1 3.22 us: on_device(): jnp.einsum('sij,qsjbc->qsibc', lat_matrix, along, preferred_element_type=...]
    unnamed x3 -> x0, waiting for transfers between devices: 8.66 us -> none
    mul x1 -> x0, other arithmetic: 2.53 us -> none  [on_device(): slab_local = betas[0] * product]
  transfers between devices with their start and end apart: 5 -> 0, of which waited for: 5 -> 0; matrix products, arithmetic and copies ran while one was open for 12% -> 0% of each run, Pallas kernels for 0% -> 0%
where the time goes in v1:
time: 61.8 us; the launch traced here: 61.5 us
  Pallas kernels  56.8 us (92%)
  local copies, waits for them, and re-layouts  3.44 us (6%)
  between operations  1.32 us (2%)
    pallas_call x1, Pallas kernels, exchange(): pl.pallas_call(exchange_kernel, out_shape=(jax.ShapeDtypeStruct((PARTS, M...  55.7 us
    unnamed x10, local copies, waits for them, and re-layouts  2.64 us

profile of v1, /device:TPU:1, one launch (start us, length us, event | category | flops | bytes accessed | tf_op | source)
XLA Modules:
  0.0 61.5 jit_solution(3898487675070654154)
XLA Ops:
  1.3 0.0 copy-start.4
  1.3 0.6 %copy-done.4 = s32[64]{0:T(128)S(1)} copy-done((s32[64]{0:T(128)S(1)}, s32[64]{0:T(128)}, u32[]{:S(2)}) %copy-start.4) | copy-done | bytes 280
  1.9 0.0 copy-start.2
  1.9 0.0 copy-start.3
  1.9 0.8 %pad.4.vertical = bf16[128,127]{1,0:T(8,128)(2,1)S(1)} pad(bf16[127,127]{1,0:T(8,128)(2,1)} %param.9, bf16[]{:T(256)} %constant.2.clone.1), padding=0_1x0_0 | pad | bytes 64772 | tf_op jit(solution)/shard_map/jit(_pad)/pad | solution.py:347
  2.7 0.0 copy-done.2
  2.7 0.0 copy-done.3
  2.8 0.0 copy-start
  2.8 1.0 %copy-done = bf16[1,127,1536]{2,1,0:T(8,128)(2,1)S(1)} copy-done((bf16[1,127,1536]{2,1,0:T(8,128)(2,1)S(1)}, bf16[1,127,1536]{2,1,0:T(8,128)(2,1)}, u32[]{:S(2)}) %copy-start) | copy-done | bytes 390168
  3.8 0.0 copy-start.1
  3.8 1.0 %copy-done.1 = bf16[1,127,1536]{2,1,0:T(8,128)(2,1)S(1)} copy-done((bf16[1,127,1536]{2,1,0:T(8,128)(2,1)S(1)}, bf16[1,127,1536]{2,1,0:T(8,128)(2,1)}, u32[]{:S(2)}) %copy-start.1) | copy-done | bytes 390168
  4.8 55.7 %exchange.1 = (bf16[3,8,8,8,128]{4,3,2,1,0:T(8,128)(2,1)S(1)}, bf16[64,8,128]{2,1,0:T(8,128)(2,1)S(1)}) custom-call(bf16[1,127,1536]{2,1,0:T(8,128)(2,1)S(1)} %copy-done, bf16[1,127,1536]{2,1,0:T(8,128)(2,1)S(1)} %copy-done.1, bf16[128,127]{1,0:T(8,128)(2,1)S(1)} %pad.4.vertical, f32[1,127]{1,0:T(1,128)S(1)} %bitcast.3, ...), custom_call_target="tpu_custom_call" | custom-call | tf_op jit(solution)/shard_map/exchange/pallas_call | solution.py:281
  60.4 1.1 %arrange.1 = (f32[127,1536]{1,0:T(8,128)}, f32[4,64,192]{2,1,0:T(8,128)}) custom-call(bf16[3,8,8,8,128]{4,3,2,1,0:T(8,128)(2,1)S(1)} %get-tuple-element.4.gathered, bf16[64,8,128]{2,1,0:T(8,128)(2,1)S(1)} %get-tuple-element.5.slab), custom_call_target="tpu_custom_call" | custom-call | tf_op jit(solution)/shard_map/arrange/pallas_call | solution.py:330
  (1 shorter events, 0.0 us)
Async XLA Ops:
  1.3 0.7 %copy-start.4 = (s32[64]{0:T(128)S(1)}, s32[64]{0:T(128)}, u32[]{:S(2)}) copy-start(s32[64]{0:T(128)} %param.11) | copy-start | bytes 772
  1.9 0.8 %copy-start.2 = (f32[127]{0:T(128)S(1)}, f32[127]{0:T(128)}, u32[]{:S(2)}) copy-start(f32[127]{0:T(128)} %param.10) | copy-start | bytes 1528
  1.9 0.8 %copy-start.3 = (f32[10]{0:T(128)S(1)}, f32[10]{0:T(128)}, u32[]{:S(2)}) copy-start(f32[10]{0:T(128)} %weights.1) | copy-start | bytes 124
  2.8 1.0 %copy-start = (bf16[1,127,1536]{2,1,0:T(8,128)(2,1)S(1)}, bf16[1,127,1536]{2,1,0:T(8,128)(2,1)}, u32[]{:S(2)}) copy-start(bf16[1,127,1536]{2,1,0:T(8,128)(2,1)} %controls.1) | copy-start | bytes 1170436
  3.8 1.0 %copy-start.1 = (bf16[1,127,1536]{2,1,0:T(8,128)(2,1)S(1)}, bf16[1,127,1536]{2,1,0:T(8,128)(2,1)}, u32[]{:S(2)}) copy-start(bf16[1,127,1536]{2,1,0:T(8,128)(2,1)} %perturb.1) | copy-start | bytes 1170436

commit v2 on v1

v2 whole, which is shorter than its diff:
```python
import jax
import jax.numpy as jnp
from jax import lax
from jax.experimental import pallas as pl
from jax.experimental.pallas import tpu as pltpu
from jax.sharding import PartitionSpec as P

LEV = 127
NLON = 1536
HALF = 24
MEM = 8
COL = 64
SIDE = 8
PARTS = 3
PAD = 32
MESH = pl.DeviceIdType.MESH
F32 = jnp.float32
BF16 = jnp.bfloat16


def taps_rows(width):
    rows = lax.broadcasted_iota(jnp.int32, (PAD, 128), 0).astype(F32)
    raw = jnp.exp(-(rows * rows) / (2.0 * width * width))
    squares = jnp.where(rows <= HALF, jnp.exp(-(rows * rows) / (width * width)), 0.0)
    normal = jnp.sqrt(2.0 * jnp.sum(squares, axis=0, keepdims=True) - 1.0)
    return (raw / normal).astype(BF16).astype(F32)


def placing_matrices(counts):
    def starts_counts(tile, rows):
        lane = lax.broadcasted_iota(jnp.int32, (rows, COL), 1)
        start = jnp.sum(jnp.where(lane < tile, counts, 0.0), axis=1, keepdims=True)
        count = jnp.sum(jnp.where(lane == tile, counts, 0.0), axis=1, keepdims=True)
        return start, count

    row = lax.broadcasted_iota(jnp.int32, (COL * 4, 1), 0)
    start, count = starts_counts(row // 4, COL * 4)
    slot = lax.rem(row, 4).astype(F32)
    target = jnp.where(slot < count, start + slot, -1.0)
    lane = lax.broadcasted_iota(jnp.int32, (COL * 4, 128), 1).astype(F32)
    first = jnp.where(lane == target, 1.0, 0.0).astype(BF16)
    row = lax.broadcasted_iota(jnp.int32, (COL * 2, 1), 0)
    start, count = starts_counts(row // 2, COL * 2)
    lane = lax.broadcasted_iota(jnp.int32, (COL * 2, 128), 1).astype(F32)
    both = []
    for odd in range(2):
        slot = (2 * lax.rem(row, 2) + odd).astype(F32)
        target = jnp.where(slot < count, start + slot, -1.0)
        both.append(jnp.where(lane == target, 1.0, 0.0).astype(BF16))
    return first, both[0], both[1]


def exchange_kernel(
    controls_hbm, perturb_hbm, vertical_hbm, scales_hbm, counts_hbm, index_hbm, weights_hbm,
    gathered_out, slab_a_out, slab_b_out,
    controls, perturb, vertical, scales, counts, index, weights,
    matrix_rows, lifted, width_row, taps, along, arrived, padded, smooth, back, columns, members,
    total, gathered, pair_a, pair_b, place_a, place_b,
    send_a, recv_a, send_b, recv_b,
    send_sems, recv_sems, load_sems,
):
    m = lax.axis_index("mem")
    c = lax.axis_index("col")
    z, y = c // SIDE, lax.rem(c, SIDE)

    loads = [
        pltpu.make_async_copy(src, dst, load_sems.at[k])
        for k, (src, dst) in enumerate(
            (
                (vertical_hbm, vertical), (controls_hbm, controls), (scales_hbm, scales),
                (counts_hbm, counts), (index_hbm, index), (weights_hbm, weights),
                (perturb_hbm, perturb),
            )
        )
    ]
    for load in loads:
        load.start()

    barrier = pltpu.get_barrier_semaphore()
    for a in (4, 3, 5, 2, 6, 1, 7, 0):
        zz = lax.rem(z + a, SIDE) * SIDE
        for b in (4, 3, 5, 2, 6, 1, 7, 0):
            if a or b:
                pl.semaphore_signal(
                    barrier, inc=1, device_id=(m, zz + lax.rem(y + b, SIDE)), device_id_type=MESH
                )
    for k in range(1, MEM):
        pl.semaphore_signal(barrier, inc=1, device_id=(lax.rem(m + k, MEM), c), device_id_type=MESH)

    matrix_rows[pl.ds(LEV, 1), :] = jnp.zeros((1, LEV), F32)
    loads[0].wait()
    matrix_rows[pl.ds(0, LEV), :] = vertical[...].astype(F32)
    filter_rows = matrix_rows[...].astype(BF16)
    loads[1].wait()
    for t in range(NLON // 128):
        block = jnp.dot(
            filter_rows, controls[0, :, pl.ds(t * 128, 128)], preferred_element_type=F32
        )
        lifted[pl.ds(PAD + t * 128, 128), :] = block.astype(BF16).astype(F32).T
    lifted[pl.ds(0, PAD), :] = lifted[pl.ds(NLON, PAD), :]
    lifted[pl.ds(PAD + NLON, PAD), :] = lifted[pl.ds(PAD, PAD), :]

    width_row[...] = jnp.full((1, 128), 16.0, F32)
    loads[2].wait()
    width_row[:, :LEV] = scales[...]
    taps[...] = taps_rows(width_row[...])
    padded[pl.ds(0, HALF)] = jnp.zeros((HALF, 8, 128), F32)
    padded[pl.ds(HALF + COL, HALF)] = jnp.zeros((HALF, 8, 128), F32)

    def weight_rows():
        return [jnp.broadcast_to(taps[k : k + 1, :], (8, 128)) for k in range(HALF + 1)]

    def send(kind, s, src, dst, device):
        pltpu.make_async_remote_copy(
            src_ref=src, dst_ref=dst,
            send_sem=send_sems.at[kind, s], recv_sem=recv_sems.at[kind, s],
            device_id=device, device_id_type=MESH,
        ).start()

    def whole(kind, s, ref, count):
        part = ref.at[s, pl.ds(0, count)]
        return pltpu.make_async_remote_copy(
            src_ref=part, dst_ref=part,
            send_sem=send_sems.at[kind, s], recv_sem=recv_sems.at[kind, s],
            device_id=(m, c), device_id_type=MESH,
        )

    def send_group(kind, s, source, dest, slot, member, group, away):
        for r in range(SIDE):
            row = group * SIDE + lax.rem(y + r, SIDE)
            if away is True:
                send(kind, s, source.at[s, row], dest.at[s, slot], (member, row))
            elif away is False:
                if r:
                    send(kind, s, source.at[s, row], dest.at[s, slot], (member, row))
            elif r == 0:
                @pl.when(away)
                def _():
                    send(kind, s, source.at[s, row], dest.at[s, slot], (member, row))
            else:
                send(kind, s, source.at[s, row], dest.at[s, slot], (member, row))

    def lon_filter(s, group):
        w = weight_rows()
        base = PAD + group * 192 + s * 64
        for b in range(SIDE):
            at = pl.multiple_of(base + 8 * b, 8)
            acc = w[0] * lifted[pl.ds(at, 8), :]
            for tap in range(1, HALF + 1):
                acc = acc + w[tap] * (lifted[pl.ds(at - tap, 8), :] + lifted[pl.ds(at + tap, 8), :])
            along[s, group * SIDE + b] = acc.astype(BF16)

    def lon_first(k, carry):
        lon_filter(0, lax.rem(z + 4 + k, SIDE))
        return carry

    lax.fori_loop(0, SIDE, lon_first, 0)
    pl.semaphore_wait(barrier, COL - 1 + MEM - 1)

    for k in range(SIDE):
        send_group(0, 0, along, arrived, c, m, lax.rem(z + 4 + k, SIDE), k != 4)

    def lon_step(it, carry):
        s, k = it // SIDE, lax.rem(it, SIDE)
        group = lax.rem(z + 4 + k, SIDE)
        lon_filter(s, group)
        send_group(0, s, along, arrived, c, m, group, k != 4)
        return carry

    lax.fori_loop(SIDE, PARTS * SIDE, lon_step, 0)

    identity = jnp.where(
        lax.broadcasted_iota(jnp.int32, (128, LEV), 0)
        == lax.broadcasted_iota(jnp.int32, (128, LEV), 1),
        1.0, 0.0,
    ).astype(BF16)
    for k in range(3, 7):
        loads[k].wait()
    beta = weights[index[0]]
    for t in range(NLON // 128):
        block = jnp.dot(identity, perturb[0, :, pl.ds(t * 128, 128)], preferred_element_type=F32)
        block = block.T.astype(BF16).reshape(2, 8, 8, 128)
        for half in range(2):
            u = 2 * t + half
            columns[0, u // 3, u % 3] = block[half]
    for k in (4, 3, 5, 2, 6, 1, 7):
        j = lax.rem(m + k, MEM)
        send(2, 0, columns.at[0, j], members.at[0, m], (j, c))
    members[0, m] = columns[0, m]
    first, even, odd = placing_matrices(counts[...].astype(F32))
    place_a[...] = first
    place_b[:, pl.ds(0, 128)] = even
    place_b[:, pl.ds(128, 128)] = odd
    pair_b[pl.ds(0, 64), pl.ds(128, 128)] = jnp.zeros((64, 128), BF16)
    pair_b[pl.ds(64, 64), pl.ds(0, 128)] = jnp.zeros((64, 128), BF16)

    here = z == m
    back_slot = m * SIDE + y
    taps[...] = taps[...] * beta

    def lat_part(s, carry):
        whole(0, s, arrived, COL - 1).wait_recv()
        arrived[s, c] = along[s, c]
        padded[pl.ds(HALF, COL)] = arrived[s].astype(F32)

        def lat_step(k, inner):
            w = weight_rows()
            group = lax.rem(z + 4 + k, SIDE)
            for r in range(SIDE):
                at = HALF + group * SIDE + r
                acc = w[0] * padded[at]
                for tap in range(1, HALF + 1):
                    acc = acc + w[tap] * (padded[at - tap] + padded[at + tap])
                smooth[s, group * SIDE + r] = acc.astype(BF16)
            send_group(
                1, s, smooth, back, back_slot, z, group,
                jnp.logical_or(k != 4, jnp.logical_not(here)),
            )
            return inner

        lax.fori_loop(0, SIDE, lat_step, 0)
        return carry

    lax.fori_loop(0, PARTS, lat_part, 0)
    whole(2, 0, members, MEM - 1).wait_recv()

    def sum_part(s):
        @pl.when(here)
        def _():
            whole(1, s, back, COL - 1).wait_recv()
            back[s, back_slot] = smooth[s, c]

        @pl.when(jnp.logical_not(here))
        def _():
            whole(1, s, back, COL).wait_recv()

        acc = jnp.zeros((8, 8, 128), F32)
        for k in range(MEM):
            acc = acc + back[s, pl.ds(k * SIDE, SIDE)].astype(F32) * members[0, k, s].astype(F32)
        total[s] = acc.astype(BF16)
        gathered[s, m] = total[s]

    def spread_part(s):
        for k in (4, 3, 5, 2, 6, 1, 7):
            send(3, s, total.at[s], gathered.at[s, m], (lax.rem(m + k, MEM), c))

    def slab_part(kind, place, pair, source, dest, rows):
        source[0] = (
            lax.dot_general(
                place[...], pair[...], (((1,), (1,)), ((), ())), preferred_element_type=F32
            )
            .astype(BF16)
            .reshape(COL, rows, 128)
        )

        for k in range(SIDE):
            group = lax.rem(z + 4 + k, SIDE)
            send_group(kind, 0, source, dest, c, m, group, k != 4)

    sum_part(0)
    spread_part(0)
    sum_part(1)
    spread_part(1)
    pair_a[pl.ds(0, 64), :] = total[0].reshape(64, 128)
    pair_a[pl.ds(64, 64), :] = total[1].reshape(64, 128)
    slab_part(4, place_a, pair_a, send_a, recv_a, 4)
    sum_part(2)
    last = total[2].reshape(64, 128)
    pair_b[pl.ds(0, 64), pl.ds(0, 128)] = last
    pair_b[pl.ds(64, 64), pl.ds(128, 128)] = last
    slab_part(5, place_b, pair_b, send_b, recv_b, 2)
    spread_part(2)

    def finish(s, carry):
        whole(3, s, gathered, MEM - 1).wait_recv()
        gathered_out[s] = gathered[s]
        whole(0, s, along, COL - 1).wait_send()

        @pl.when(here)
        def _():
            whole(1, s, smooth, COL - 1).wait_send()

        @pl.when(jnp.logical_not(here))
        def _():
            whole(1, s, smooth, COL).wait_send()

        whole(3, s, gathered, MEM - 1).wait_send()
        return carry

    lax.fori_loop(0, PARTS, finish, 0)
    whole(2, 0, columns, MEM - 1).wait_send()
    whole(4, 0, recv_a, COL - 1).wait_recv()
    recv_a[0, c] = send_a[0, c]
    slab_a_out[...] = recv_a[0]
    whole(5, 0, recv_b, COL - 1).wait_recv()
    recv_b[0, c] = send_b[0, c]
    slab_b_out[...] = recv_b[0]
    whole(4, 0, send_a, COL - 1).wait_send()
    whole(5, 0, send_b, COL - 1).wait_send()


def exchange(controls, perturb, vertical, scales, counts, index, weights):
    block = (8, 128)
    vmem = pl.BlockSpec(memory_space=pltpu.VMEM)
    hbm = pl.BlockSpec(memory_space=pl.ANY)
    return pl.pallas_call(
        exchange_kernel,
        out_shape=(
            jax.ShapeDtypeStruct((PARTS, MEM, 8) + block, BF16),
            jax.ShapeDtypeStruct((COL, 4, 128), BF16),
            jax.ShapeDtypeStruct((COL, 2, 128), BF16),
        ),
        in_specs=[hbm] * 7,
        out_specs=(vmem, vmem, vmem),
        scratch_shapes=[
            pltpu.VMEM((1, LEV, NLON), BF16),
            pltpu.VMEM((1, LEV, NLON), BF16),
            pltpu.VMEM((LEV, LEV), BF16),
            pltpu.VMEM((1, LEV), F32),
            pltpu.VMEM((1, COL), jnp.int32),
            pltpu.SMEM((1,), jnp.int32),
            pltpu.SMEM((10,), F32),
            pltpu.VMEM((128, LEV), F32),
            pltpu.VMEM((PAD + NLON + PAD, 128), F32),
            pltpu.VMEM((1, 128), F32),
            pltpu.VMEM((PAD, 128), F32),
            pltpu.VMEM((PARTS, COL) + block, BF16),
            pltpu.VMEM((PARTS, COL) + block, BF16),
            pltpu.VMEM((HALF + COL + HALF,) + block, F32),
            pltpu.VMEM((PARTS, COL) + block, BF16),
            pltpu.VMEM((PARTS, COL) + block, BF16),
            pltpu.VMEM((1, MEM, PARTS, 8) + block, BF16),
            pltpu.VMEM((1, MEM, PARTS, 8) + block, BF16),
            pltpu.VMEM((PARTS, 8) + block, BF16),
            pltpu.VMEM((PARTS, MEM, 8) + block, BF16),
            pltpu.VMEM((128, 128), BF16),
            pltpu.VMEM((128, 256), BF16),
            pltpu.VMEM((COL * 4, 128), BF16),
            pltpu.VMEM((COL * 2, 256), BF16),
            pltpu.VMEM((1, COL, 4, 128), BF16),
            pltpu.VMEM((1, COL, 4, 128), BF16),
            pltpu.VMEM((1, COL, 2, 128), BF16),
            pltpu.VMEM((1, COL, 2, 128), BF16),
            pltpu.SemaphoreType.DMA((6, PARTS)),
            pltpu.SemaphoreType.DMA((6, PARTS)),
            pltpu.SemaphoreType.DMA((7,)),
        ],
        compiler_params=pltpu.CompilerParams(
            collective_id=0, has_side_effects=True, vmem_limit_bytes=32 * 1024 * 1024
        ),
        name="exchange",
    )(
        *(
            pltpu.with_memory_space_constraint(x, pltpu.HBM)
            for x in (controls, perturb, vertical, scales, counts)
        ),
        index, pltpu.with_memory_space_constraint(weights, pltpu.HBM),
    )


def arrange_kernel(gathered, slab_a, slab_b, increment, slab_increment, rows_a, rows_b):
    for t in range(NLON // 128):
        halves = [gathered[u % 3, u // 3].astype(F32).reshape(64, 128) for u in (2 * t, 2 * t + 1)]
        block = jnp.concatenate(halves, axis=0).T
        increment[:, pl.ds(t * 128, 128)] = block[:LEV]
    rows_a[...] = slab_a[...].astype(F32).reshape(COL * 4, 128)
    rows_b[...] = slab_b[...].astype(F32).reshape(COL * 2, 128)
    for q in range(4):
        slab_increment[q, :, pl.ds(0, 128)] = rows_a[pl.ds(q, COL, stride=4), :]
    for r in range(2):
        both = rows_b[pl.ds(r, COL, stride=2), :]
        slab_increment[2 * r, :, pl.ds(128, 64)] = both[:, :64]
        slab_increment[2 * r + 1, :, pl.ds(128, 64)] = both[:, 64:]


def arrange(gathered, slab_a, slab_b):
    vmem = pl.BlockSpec(memory_space=pltpu.VMEM)
    return pl.pallas_call(
        arrange_kernel,
        out_shape=(
            jax.ShapeDtypeStruct((LEV, NLON), F32),
            jax.ShapeDtypeStruct((4, COL, 192), F32),
        ),
        in_specs=[vmem, vmem, vmem],
        out_specs=(vmem, vmem),
        scratch_shapes=[pltpu.VMEM((COL * 4, 128), F32), pltpu.VMEM((COL * 2, 128), F32)],
        compiler_params=pltpu.CompilerParams(vmem_limit_bytes=16 * 1024 * 1024),
        name="arrange",
    )(gathered, slab_a, slab_b)


def on_device(
    controls, perturbations, vertical_filter, scales, level_counts, weight_index, member_weights
):
    outs = exchange(
        controls, perturbations, vertical_filter, scales[None, :],
        level_counts[None, :], weight_index, member_weights,
    )
    return arrange(*outs)


def solution(mesh):
    return jax.shard_map(
        on_device,
        mesh=mesh,
        in_specs=(P("mem", None, "col"), P("mem", None, "col"), P(), P(), P(), P("mem"), P()),
        out_specs=(P(None, "col"), P("col", None, "mem")),
        check_vma=False,
    )
```

time: 61.8 us -> 50.7 us (0.82)
  Pallas kernels: 56.8 us -> 49.3 us
  local copies, waits for them, and re-layouts: 3.44 us -> 0 us
    pallas_call x1, Pallas kernels: 55.7 us -> 48.2 us  [exchange(): pl.pallas_call(exchange_kernel, out_shape=(jax.ShapeDtypeStruct((PARTS, M...]
    unnamed x10 -> x0, local copies, waits for them, and re-layouts: 2.64 us -> none
    pad x1 -> x0, local copies, waits for them, and re-layouts: 0.79 us -> none  [on_device(): vertical = jnp.pad(vertical_filter, ((0, 1), (0, 0)))]
where the time goes in v2:
time: 50.7 us; the launch traced here: 50.6 us
  Pallas kernels  49.3 us (97%)
  between operations  1.29 us (3%)
    pallas_call x1, Pallas kernels, exchange(): pl.pallas_call(exchange_kernel, out_shape=(jax.ShapeDtypeStruct((PARTS, M...  48.2 us
    pallas_call x1, Pallas kernels, arrange(): pl.pallas_call(arrange_kernel, out_shape=(jax.ShapeDtypeStruct((LEV, NLON...  1.15 us

profile of v2, /device:TPU:1, one launch (start us, length us, event | category | flops | bytes accessed | tf_op | source)
XLA Modules:
  0.0 50.6 jit_solution(4154933314845510944)
XLA Ops:
  1.3 48.2 %exchange.1 = (bf16[3,8,8,8,128]{4,3,2,1,0:T(8,128)(2,1)S(1)}, bf16[64,4,128]{2,1,0:T(4,128)(2,1)S(1)}, bf16[64,2,128]{2,1,0:T(2,128)(2,1)S(1)}) custom-call(bf16[1,127,1536]{2,1,0:T(8,128)(2,1)} %controls_hbm.1, bf16[1,127,1536]{2,1,0:T(8,128)(2,1)} %perturb_hbm.1, bf16[127,127]{1,0:T(8,128)(2,1)} %vertical_hbm.1, f32[1,127]{1,0:T(1,128)} %bitcast.2, ...), custom_call_target="tpu_custom_call" | custom-call | tf_op jit(solution)/shard_map/exchange/pallas_call | solution.py:306
  49.4 1.2 %arrange.1 = (f32[127,1536]{1,0:T(8,128)}, f32[4,64,192]{2,1,0:T(8,128)}) custom-call(bf16[3,8,8,8,128]{4,3,2,1,0:T(8,128)(2,1)S(1)} %get-tuple-element.5.gathered, bf16[64,4,128]{2,1,0:T(4,128)(2,1)S(1)} %get-tuple-element.6.slab_a, bf16[64,2,128]{2,1,0:T(2,128)(2,1)S(1)} %get-tuple-element.7.slab_b), custom_call_target="tpu_custom_call" | custom-call | tf_op jit(solution)/shard_map/arrange/pallas_call | solution.py:378

commit v3 on v2

--- a/solution.py
+++ b/solution.py
@@ -14,6 +14,7 @@
 PARTS = 3
 PAD = 32
 MESH = pl.DeviceIdType.MESH
+FAR_FIRST = (4, 3, 5, 2, 6, 1, 7, 0)
 F32 = jnp.float32
 BF16 = jnp.bfloat16
 
@@ -52,7 +53,7 @@
 
 def exchange_kernel(
     controls_hbm, perturb_hbm, vertical_hbm, scales_hbm, counts_hbm, index_hbm, weights_hbm,
-    gathered_out, slab_a_out, slab_b_out,
+    increment_out, slab_a_out, slab_b_out,
     controls, perturb, vertical, scales, counts, index, weights,
     matrix_rows, lifted, width_row, taps, along, arrived, padded, smooth, back, columns, members,
     total, gathered, pair_a, pair_b, place_a, place_b,
@@ -77,9 +78,9 @@
         load.start()
 
     barrier = pltpu.get_barrier_semaphore()
-    for a in (4, 3, 5, 2, 6, 1, 7, 0):
+    for a in FAR_FIRST:
         zz = lax.rem(z + a, SIDE) * SIDE
-        for b in (4, 3, 5, 2, 6, 1, 7, 0):
+        for b in FAR_FIRST:
             if a or b:
                 pl.semaphore_signal(
                     barrier, inc=1, device_id=(m, zz + lax.rem(y + b, SIDE)), device_id_type=MESH
@@ -126,19 +127,17 @@
         )
 
     def send_group(kind, s, source, dest, slot, member, group, away):
-        for r in range(SIDE):
-            row = group * SIDE + lax.rem(y + r, SIDE)
-            if away is True:
+        for b in FAR_FIRST:
+            row = group * SIDE + lax.rem(y + b, SIDE)
+            if b or away is True:
                 send(kind, s, source.at[s, row], dest.at[s, slot], (member, row))
-            elif away is False:
-                if r:
-                    send(kind, s, source.at[s, row], dest.at[s, slot], (member, row))
-            elif r == 0:
+            elif away is not False:
                 @pl.when(away)
                 def _():
                     send(kind, s, source.at[s, row], dest.at[s, slot], (member, row))
-            else:
-                send(kind, s, source.at[s, row], dest.at[s, slot], (member, row))
+
+    def group_at(k):
+        return lax.rem(z + 4 + (1 - 2 * lax.rem(k, 2)) * ((k + 1) // 2), SIDE)
 
     def lon_filter(s, group):
         w = weight_rows()
@@ -151,20 +150,20 @@
             along[s, group * SIDE + b] = acc.astype(BF16)
 
     def lon_first(k, carry):
-        lon_filter(0, lax.rem(z + 4 + k, SIDE))
+        lon_filter(0, group_at(k))
         return carry
 
     lax.fori_loop(0, SIDE, lon_first, 0)
     pl.semaphore_wait(barrier, COL - 1 + MEM - 1)
 
-    for k in range(SIDE):
-        send_group(0, 0, along, arrived, c, m, lax.rem(z + 4 + k, SIDE), k != 4)
+    for a in FAR_FIRST:
+        send_group(0, 0, along, arrived, c, m, lax.rem(z + a, SIDE), a != 0)
 
     def lon_step(it, carry):
         s, k = it // SIDE, lax.rem(it, SIDE)
-        group = lax.rem(z + 4 + k, SIDE)
+        group = group_at(k)
         lon_filter(s, group)
-        send_group(0, s, along, arrived, c, m, group, k != 4)
+        send_group(0, s, along, arrived, c, m, group, k != SIDE - 1)
         return carry
 
     lax.fori_loop(SIDE, PARTS * SIDE, lon_step, 0)
@@ -205,7 +204,7 @@
 
         def lat_step(k, inner):
             w = weight_rows()
-            group = lax.rem(z + 4 + k, SIDE)
+            group = group_at(k)
             for r in range(SIDE):
                 at = HALF + group * SIDE + r
                 acc = w[0] * padded[at]
@@ -214,7 +213,7 @@
                 smooth[s, group * SIDE + r] = acc.astype(BF16)
             send_group(
                 1, s, smooth, back, back_slot, z, group,
-                jnp.logical_or(k != 4, jnp.logical_not(here)),
+                jnp.logical_or(k != SIDE - 1, jnp.logical_not(here)),
             )
             return inner
 
@@ -253,9 +252,8 @@
             .reshape(COL, rows, 128)
         )
 
-        for k in range(SIDE):
-            group = lax.rem(z + 4 + k, SIDE)
-            send_group(kind, 0, source, dest, c, m, group, k != 4)
+        for a in FAR_FIRST:
+            send_group(kind, 0, source, dest, c, m, lax.rem(z + a, SIDE), a != 0)
 
     sum_part(0)
     spread_part(0)
@@ -273,7 +271,6 @@
 
     def finish(s, carry):
         whole(3, s, gathered, MEM - 1).wait_recv()
-        gathered_out[s] = gathered[s]
         whole(0, s, along, COL - 1).wait_send()
 
         @pl.when(here)
@@ -288,6 +285,9 @@
         return carry
 
     lax.fori_loop(0, PARTS, finish, 0)
+    for t in range(NLON // 128):
+        halves = [gathered[u % 3, u // 3].astype(F32).reshape(64, 128) for u in (2 * t, 2 * t + 1)]
+        increment_out[:, pl.ds(t * 128, 128)] = jnp.concatenate(halves, axis=0).T[:LEV]
     whole(2, 0, columns, MEM - 1).wait_send()
     whole(4, 0, recv_a, COL - 1).wait_recv()
     recv_a[0, c] = send_a[0, c]
@@ -306,7 +306,7 @@
     return pl.pallas_call(
         exchange_kernel,
         out_shape=(
-            jax.ShapeDtypeStruct((PARTS, MEM, 8) + block, BF16),
+            jax.ShapeDtypeStruct((LEV, NLON), F32),
             jax.ShapeDtypeStruct((COL, 4, 128), BF16),
             jax.ShapeDtypeStruct((COL, 2, 128), BF16),
         ),
@@ -358,23 +358,26 @@
     )
 
 
-def arrange_kernel(gathered, slab_a, slab_b, increment, slab_increment, rows_a, rows_b):
-    for t in range(NLON // 128):
-        halves = [gathered[u % 3, u // 3].astype(F32).reshape(64, 128) for u in (2 * t, 2 * t + 1)]
-        block = jnp.concatenate(halves, axis=0).T
-        increment[:, pl.ds(t * 128, 128)] = block[:LEV]
+def arrange_kernel(ready, slab_a, slab_b, increment, slab_increment, rows_a, rows_b, slots, sems):
+    whole = pltpu.make_async_copy(ready, increment, sems.at[0])
+    whole.start()
     rows_a[...] = slab_a[...].astype(F32).reshape(COL * 4, 128)
     rows_b[...] = slab_b[...].astype(F32).reshape(COL * 2, 128)
     for q in range(4):
-        slab_increment[q, :, pl.ds(0, 128)] = rows_a[pl.ds(q, COL, stride=4), :]
+        slots[q, :, pl.ds(0, 128)] = rows_a[pl.ds(q, COL, stride=4), :]
     for r in range(2):
         both = rows_b[pl.ds(r, COL, stride=2), :]
-        slab_increment[2 * r, :, pl.ds(128, 64)] = both[:, :64]
-        slab_increment[2 * r + 1, :, pl.ds(128, 64)] = both[:, 64:]
-
-
-def arrange(gathered, slab_a, slab_b):
+        slots[2 * r, :, pl.ds(128, 64)] = both[:, :64]
+        slots[2 * r + 1, :, pl.ds(128, 64)] = both[:, 64:]
+    owned = pltpu.make_async_copy(slots, slab_increment, sems.at[1])
+    owned.start()
+    whole.wait()
+    owned.wait()
+
+
+def arrange(ready, slab_a, slab_b):
     vmem = pl.BlockSpec(memory_space=pltpu.VMEM)
+    hbm = pl.BlockSpec(memory_space=pl.ANY)
     return pl.pallas_call(
         arrange_kernel,
         out_shape=(
@@ -382,11 +385,16 @@
             jax.ShapeDtypeStruct((4, COL, 192), F32),
         ),
         in_specs=[vmem, vmem, vmem],
-        out_specs=(vmem, vmem),
-        scratch_shapes=[pltpu.VMEM((COL * 4, 128), F32), pltpu.VMEM((COL * 2, 128), F32)],
+        out_specs=(hbm, hbm),
+        scratch_shapes=[
+            pltpu.VMEM((COL * 4, 128), F32),
+            pltpu.VMEM((COL * 2, 128), F32),
+            pltpu.VMEM((4, COL, 192), F32),
+            pltpu.SemaphoreType.DMA((2,)),
+        ],
         compiler_params=pltpu.CompilerParams(vmem_limit_bytes=16 * 1024 * 1024),
         name="arrange",
-    )(gathered, slab_a, slab_b)
+    )(ready, slab_a, slab_b)
 
 
 def on_device(

time: 50.7 us -> 49.3 us (0.972)
  Pallas kernels: 49.3 us -> 47.9 us
    pallas_call x1, Pallas kernels: 48.2 us -> 46.9 us  [exchange(): pl.pallas_call(exchange_kernel, out_shape=(jax.ShapeDtypeStruct((LEV, NLO...]
where the time goes in v3:
time: 49.3 us; the launch traced here: 49.2 us
  Pallas kernels  47.9 us (97%)
  between operations  1.29 us (3%)
    pallas_call x1, Pallas kernels, exchange(): pl.pallas_call(exchange_kernel, out_shape=(jax.ShapeDtypeStruct((LEV, NLO...  46.9 us
    pallas_call x1, Pallas kernels, arrange(): pl.pallas_call(arrange_kernel, out_shape=(jax.ShapeDtypeStruct((LEV, NLON...  0.99 us

profile of v3, /device:TPU:1, one launch (start us, length us, event | category | flops | bytes accessed | tf_op | source)
XLA Modules:
  0.0 49.2 jit_solution(6730400695534799596)
XLA Ops:
  1.3 46.9 %exchange.1 = (f32[127,1536]{1,0:T(8,128)S(1)}, bf16[64,4,128]{2,1,0:T(4,128)(2,1)S(1)}, bf16[64,2,128]{2,1,0:T(2,128)(2,1)S(1)}) custom-call(bf16[1,127,1536]{2,1,0:T(8,128)(2,1)} %controls_hbm.1, bf16[1,127,1536]{2,1,0:T(8,128)(2,1)} %perturb_hbm.1, bf16[127,127]{1,0:T(8,128)(2,1)} %vertical_hbm.1, f32[1,127]{1,0:T(1,128)} %bitcast.2, s32[1,64]{1,0:T(1,128)} %bitcast.3, ...), custom_call_target="tpu_custom_call" | custom-call | tf_op jit(solution)/shard_map/exchange/pallas_call | solution.py:306
  48.2 1.0 %arrange.1 = (f32[127,1536]{1,0:T(8,128)}, f32[4,64,192]{2,1,0:T(8,128)}) custom-call(f32[127,1536]{1,0:T(8,128)S(1)} %get-tuple-element.5.ready, bf16[64,4,128]{2,1,0:T(4,128)(2,1)S(1)} %get-tuple-element.6.slab_a, bf16[64,2,128]{2,1,0:T(2,128)(2,1)S(1)} %get-tuple-element.7.slab_b), custom_call_target="tpu_custom_call" | custom-call | tf_op jit(solution)/shard_map/arrange/pallas_call | solution.py:381

commit v4 on v3

--- a/solution.py
+++ b/solution.py
@@ -142,11 +142,14 @@
     def lon_filter(s, group):
         w = weight_rows()
         base = PAD + group * 192 + s * 64
+        at = pl.multiple_of(base, 8)
         for b in range(SIDE):
-            at = pl.multiple_of(base + 8 * b, 8)
-            acc = w[0] * lifted[pl.ds(at, 8), :]
+            mid = at + 8 * b
+            acc = w[0] * lifted[pl.ds(mid, 8), :]
             for tap in range(1, HALF + 1):
-                acc = acc + w[tap] * (lifted[pl.ds(at - tap, 8), :] + lifted[pl.ds(at + tap, 8), :])
+                acc = acc + w[tap] * (
+                    lifted[pl.ds(mid - tap, 8), :] + lifted[pl.ds(mid + tap, 8), :]
+                )
             along[s, group * SIDE + b] = acc.astype(BF16)
 
     def lon_first(k, carry):
@@ -205,12 +208,17 @@
         def lat_step(k, inner):
             w = weight_rows()
             group = group_at(k)
-            for r in range(SIDE):
+            for r in range(0, SIDE, 4):
                 at = HALF + group * SIDE + r
-                acc = w[0] * padded[at]
+                low = [padded[at + i] for i in range(4)]
+                high = low
+                acc = [w[0] * value for value in low]
                 for tap in range(1, HALF + 1):
-                    acc = acc + w[tap] * (padded[at - tap] + padded[at + tap])
-                smooth[s, group * SIDE + r] = acc.astype(BF16)
+                    low = [padded[at - tap]] + low[:3]
+                    high = high[1:] + [padded[at + 3 + tap]]
+                    acc = [a + w[tap] * (p + q) for a, p, q in zip(acc, low, high)]
+                for i in range(4):
+                    smooth[s, group * SIDE + r + i] = acc[i].astype(BF16)
             send_group(
                 1, s, smooth, back, back_slot, z, group,
                 jnp.logical_or(k != SIDE - 1, jnp.logical_not(here)),

time: 49.3 us -> 49.4 us (level)
  no operation moved by 1% of the time
where the time goes in v4:
time: 49.4 us; the launch traced here: 49.2 us
  Pallas kernels  47.9 us (97%)
  between operations  1.29 us (3%)
    pallas_call x1, Pallas kernels, exchange(): pl.pallas_call(exchange_kernel, out_shape=(jax.ShapeDtypeStruct((LEV, NLO...  46.9 us
    pallas_call x1, Pallas kernels, arrange(): pl.pallas_call(arrange_kernel, out_shape=(jax.ShapeDtypeStruct((LEV, NLON...  0.99 us

profile of v4, /device:TPU:1, one launch (start us, length us, event | category | flops | bytes accessed | tf_op | source)
XLA Modules:
  0.0 49.2 jit_solution(17975938414216159881)
XLA Ops:
  1.3 46.9 %exchange.1 = (f32[127,1536]{1,0:T(8,128)S(1)}, bf16[64,4,128]{2,1,0:T(4,128)(2,1)S(1)}, bf16[64,2,128]{2,1,0:T(2,128)(2,1)S(1)}) custom-call(bf16[1,127,1536]{2,1,0:T(8,128)(2,1)} %controls_hbm.1, bf16[1,127,1536]{2,1,0:T(8,128)(2,1)} %perturb_hbm.1, bf16[127,127]{1,0:T(8,128)(2,1)} %vertical_hbm.1, f32[1,127]{1,0:T(1,128)} %bitcast.2, s32[1,64]{1,0:T(1,128)} %bitcast.3, ...), custom_call_target="tpu_custom_call" | custom-call | tf_op jit(solution)/shard_map/exchange/pallas_call | solution.py:314
  48.2 1.0 %arrange.1 = (f32[127,1536]{1,0:T(8,128)}, f32[4,64,192]{2,1,0:T(8,128)}) custom-call(f32[127,1536]{1,0:T(8,128)S(1)} %get-tuple-element.5.ready, bf16[64,4,128]{2,1,0:T(4,128)(2,1)S(1)} %get-tuple-element.6.slab_a, bf16[64,2,128]{2,1,0:T(2,128)(2,1)S(1)} %get-tuple-element.7.slab_b), custom_call_target="tpu_custom_call" | custom-call | tf_op jit(solution)/shard_map/arrange/pallas_call | solution.py:389
